TPU v7x, 512 devices: a whole 4x4x16 slice. The times are simulated.
512 devices in a mesh: dp: 64 (over y, z), mp: 8 (over x, core).
Axes of the slice: x: 4, y: 4, z: 16, core: 2. Of those that a mesh axis runs over, the one named last changes fastest.
Arguments:
- picks: int32 [64, 16], P('dp'), may hold values from 0 to 511, as said below
- query_embed: bfloat16 [64, 768], P('dp')
- dec_queries: bfloat16 [64, 8, 2048], P('dp')
- passage_states: bfloat16 [512, 32, 4096], P('dp', None, 'mp'), may hold values from -6 to 6
- retr_states: bfloat16 [512, 32, 768], P('dp', 'mp'), may hold values from -6 to 6
- key_weight: bfloat16 [4096, 2048], P(None, 'mp'), may hold values from -0.09375 to 0.09375
- retr_weight: bfloat16 [768, 768], replicated, may hold values from -0.21875 to 0.21875
Outputs:
- grad_embed: float32 [512, 768], P('dp')
- grad_query: float32 [64, 768], P('dp')
Inputs may be any that keep to these rules, and one draw needn't show every extreme that they name: `picks`: the owner shard of passage id p is p // 8. Among the 16 ids of the queries of one index of dp, at most 2 lie on any one owner shard, repeats counted, and some owner shard holds exactly 2 of them for every index of dp. Some owner shards are picked far more often than others.
All inputs are finite; a program needn't handle non-finite values.
Results may differ from a plain program's by a relative error of at most 0.007.
Values may be sent and summed in bfloat16 or wider, within the bound.
A program may use at most 64 MiB of HBM per device.

v0:
```python
import jax
import jax.numpy as jnp
from jax import lax
from jax.sharding import PartitionSpec as P

HD = 64
CAP = 2


def body(picks, query_embed, dec_queries, passage_states, retr_states, key_weight, retr_weight):
    shards = lax.axis_size("dp")
    width_parts = lax.axis_size("mp")
    q_dev, cands = picks.shape
    p_dev, length, width_part = passage_states.shape
    token_part = retr_states.shape[1]
    retr_width = retr_weight.shape[0]
    answers = dec_queries.shape[1]
    all_cols = dec_queries.shape[2]
    heads = all_cols // HD
    local_heads = heads // width_parts
    count = q_dev * cands
    seq_len = cands * length
    flat_ids = picks.reshape(count)
    owner_ids = flat_ids // p_dev
    local_ids = flat_ids - owner_ids * p_dev
    positions = jnp.arange(count, dtype=jnp.int32)
    earlier = (owner_ids[:, None] == owner_ids[None, :]) & (positions[None, :] < positions[:, None])
    slot_rank = jnp.sum(earlier.astype(jnp.int32), axis=1)
    slot_ids = owner_ids * CAP + slot_rank
    requests = (
        jnp.full((shards * CAP,), -1, jnp.int32).at[slot_ids].set(local_ids).reshape(shards, CAP)
    )
    received = lax.all_to_all(requests, "dp", split_axis=0, concat_axis=0, tiled=True)
    wanted = jnp.maximum(received, 0)
    states = jnp.take(passage_states, wanted, axis=0)
    back_states = lax.all_to_all(states, "dp", split_axis=0, concat_axis=0, tiled=True)
    tokens = jnp.take(retr_states, wanted, axis=0)
    back_retr = lax.all_to_all(tokens, "dp", split_axis=0, concat_axis=0, tiled=True)
    pick_states = jnp.take(back_states.reshape(shards * CAP, length, width_part), slot_ids, axis=0)
    pick_tokens = jnp.take(
        back_retr.reshape(shards * CAP, token_part, retr_width), slot_ids, axis=0
    )
    pooled_part = jnp.sum(pick_tokens.astype(jnp.float32), axis=1)
    local_cols = key_weight.shape[1]
    piece = lax.all_gather(pick_states, "mp", axis=2, tiled=True)
    flat_piece = piece.reshape(count * length, piece.shape[2])
    keys = jnp.dot(flat_piece, key_weight, preferred_element_type=jnp.float32)
    first_col = lax.axis_index("mp") * local_cols
    local_dec = lax.dynamic_slice_in_dim(dec_queries, first_col, local_cols, 2)
    local_dec = local_dec.astype(jnp.float32).reshape(q_dev, answers, local_heads, HD)
    keys = keys.reshape(q_dev, seq_len, local_heads, HD)
    scores = jnp.einsum("qahd,qshd->qahs", local_dec, keys, precision=lax.Precision.HIGHEST)
    attn = jax.nn.softmax(scores, axis=-1)
    mass_part = jnp.sum(
        attn.reshape(q_dev, answers, local_heads, cands, length), axis=(1, 2, 4)
    ) / (answers * heads)
    mass, pooled = lax.psum((mass_part, pooled_part), "mp")
    pooled_short = (pooled / length).astype(jnp.bfloat16)
    embeds = jnp.dot(pooled_short, retr_weight, preferred_element_type=jnp.float32).reshape(
        q_dev, cands, retr_width
    )
    query_full = query_embed.astype(jnp.float32)
    retr_scores = jnp.einsum("qkr,qr->qk", embeds, query_full, precision=lax.Precision.HIGHEST)
    retr_probs = jax.nn.softmax(retr_scores, axis=-1)
    delta = retr_probs - mass
    grad_query = jnp.einsum("qk,qkr->qr", delta, embeds, precision=lax.Precision.HIGHEST)
    grad_each = (delta[:, :, None] * query_full[:, None, :]).reshape(count, retr_width)
    outgoing = jnp.zeros((shards * CAP, retr_width), jnp.float32).at[slot_ids].set(grad_each)
    incoming = lax.all_to_all(
        outgoing.reshape(shards, CAP, retr_width), "dp", split_axis=0, concat_axis=0, tiled=True
    )
    matches = (
        received.reshape(shards * CAP)[:, None] == jnp.arange(p_dev, dtype=jnp.int32)[None, :]
    ).astype(jnp.float32)
    grad_embed = jnp.dot(
        matches.T,
        incoming.reshape(shards * CAP, retr_width),
        precision=lax.Precision.HIGHEST,
        preferred_element_type=jnp.float32,
    )
    return (grad_embed, grad_query)


def solution(mesh):
    placed = (
        P("dp", None),
        P("dp", None),
        P("dp", None, None),
        P("dp", None, "mp"),
        P("dp", "mp", None),
        P(None, "mp"),
        P(),
    )
    return jax.shard_map(
        body, mesh=mesh, in_specs=placed, out_specs=(P("dp", None), P("dp", None)), check_vma=False
    )
```

profile of v0, /device:TPU:1, one launch (start us, length us, event | category | flops | bytes accessed | tf_op | source)
XLA Modules:
  0.0 373.6 jit_solution(3277827031348976088)
XLA Ops:
  7.2 0.8 bitcast_subtract_fusion.1
  10.2 32.4 %all_to_all.24 = s32[64,1,2]{2,1,0:T(1,128)S(1)} all-to-all(s32[64,1,2]{2,1,0:T(1,128)S(1)} %bitcast.69), channel_id=1, replica_groups=mesh['dp'=64,'mp'=8] {'dp'}, dimensions={0} | all-to-all | bytes 1024 | tf_op jit(solution)/shard_map/all_to_all | solution.py:33
  43.1 0.8 fusion.21
  44.4 3.7 %gather_fusion.2 = bf16[128,32,512]{2,1,0:T(8,128)(2,1)} fusion(bf16[8,32,512]{2,1,0:T(8,128)(2,1)} %param.10, s32[1024]{0:T(1024)S(1)} %pad_clamp_fusion.1), kind=kCustom, calls=%fused_computation.2 | custom fusion | bytes 8389120 | tf_op jit(solution)/shard_map/jit(_take)/gather | solution.py:35
  48.1 4.6 %broadcast_select_fusion = bf16[64,2,32,512]{3,2,1,0:T(8,128)(2,1)} fusion(bf16[64,2,32,512]{3,2,1,0:T(8,128)(2,1)} %bitcast.66, pred[64,2]{1,0:T(8,128)(4,1)S(1)} %copy.25), kind=kLoop, calls=%fused_computation.6 | loop fusion | flops 2097152 | bytes 8388736 | tf_op jit(solution)/shard_map/jit(_take)/select_n | solution.py:35
  52.7 5.8 %all-to-all-start.2 = ((bf16[64,2,32,512]{3,2,1,0:T(8,128)(2,1)}), bf16[64,2,32,512]{3,2,1,0:T(8,128)(2,1)}, u32[]{:S(2)}, u32[]{:S(2)}) async-start(bf16[64,2,32,512]{3,2,1,0:T(8,128)(2,1)} %broadcast_select_fusion), calls=%async_computation.2 | async-start | bytes 8388608 | tf_op jit(solution)/shard_map/all_to_all | solution.py:36
  58.6 181.5 %all-to-all-done.2 = bf16[64,2,32,512]{3,2,1,0:T(8,128)(2,1)} async-done(((bf16[64,2,32,512]{3,2,1,0:T(8,128)(2,1)}), bf16[64,2,32,512]{3,2,1,0:T(8,128)(2,1)}, u32[]{:S(2)}, u32[]{:S(2)}) %all-to-all-start.2) | async-done | bytes 4194336 | tf_op jit(solution)/shard_map/all_to_all | solution.py:36
  240.0 2.8 gather_fusion.3
  242.8 0.9 broadcast_select_fusion.2
  243.8 1.3 gather_fusion
  245.1 1.4 broadcast_select_fusion.1
  246.4 14.1 %all-to-all-start.1 = ((bf16[64,2,4,768]{3,2,1,0:T(4,128)(2,1)}), bf16[64,2,4,768]{3,2,1,0:T(4,128)(2,1)}, u32[]{:S(2)}, u32[]{:S(2)}) async-start(bf16[64,2,4,768]{3,2,1,0:T(4,128)(2,1)} %broadcast_select_fusion.1), calls=%async_computation.1 | async-start | bytes 1572864 | tf_op jit(solution)/shard_map/all_to_all | solution.py:38
  260.5 3.0 copy.27
  264.4 35.9 %all-to-all-done.1 = bf16[64,2,4,768]{3,2,1,0:T(4,128)(2,1)} async-done(((bf16[64,2,4,768]{3,2,1,0:T(4,128)(2,1)}), bf16[64,2,4,768]{3,2,1,0:T(4,128)(2,1)}, u32[]{:S(2)}, u32[]{:S(2)}) %all-to-all-start.1) | async-done | bytes 786464 | tf_op jit(solution)/shard_map/all_to_all | solution.py:38
  300.3 1.8 gather_fusion.1
  302.3 3.5 fusion.24
  306.6 24.7 %all-reduce = (f32[1,16]{1,0:T(1,128)S(1)}, f32[16,768]{1,0:T(8,128)S(1)}) all-reduce(f32[1,16]{1,0:T(1,128)S(1)} %multiply_bitcast_fusion, f32[16,768]{1,0:T(8,128)S(1)} %convert_reduce_fusion), channel_id=1, replica_groups=mesh['dp'=64,'mp'=8] {'mp'}, use_global_device_ids=true, to_apply=%region_10.11 | all-reduce | flops 12304 | bytes 98432 | tf_op jit(solution)/shard_map/psum | solution.py:57
  332.4 1.2 fusion.20
  333.7 1.3 bitcast_subtract_fusion
  335.0 0.8 scatter_custom_fusion.1
  335.8 1.0 reshape.251
  336.8 7.8 %all-to-all-start.3 = ((f32[64,2,768]{2,1,0:T(2,128)}), f32[64,2,768]{2,1,0:T(2,128)S(1)}, u32[]{:S(2)}, u32[]{:S(2)}) async-start(f32[64,2,768]{2,1,0:T(2,128)} %reshape.251), calls=%async_computation.3 | async-start | bytes 786432 | tf_op jit(solution)/shard_map/all_to_all | solution.py:69
  345.5 20.1 %all-to-all-done.3 = f32[64,2,768]{2,1,0:T(2,128)S(1)} async-done(((f32[64,2,768]{2,1,0:T(2,128)}), f32[64,2,768]{2,1,0:T(2,128)S(1)}, u32[]{:S(2)}, u32[]{:S(2)}) %all-to-all-start.3) | async-done | bytes 393248 | tf_op jit(solution)/shard_map/all_to_all | solution.py:69
  365.9 0.9 fusion.2
  (38 shorter events, 7.4 us)
Async XLA Ops:
  7.2 324.2 %copy-start = (bf16[768,768]{1,0:T(8,128)(2,1)S(1)}, bf16[768,768]{1,0:T(8,128)(2,1)}, u32[]{:S(2)}) copy-start(bf16[768,768]{1,0:T(8,128)(2,1)} %param.13) | copy-start | bytes 3538948
  52.7 191.1 %copy-start.1 = (bf16[8,4,768]{2,1,0:T(4,128)(2,1)S(1)}, bf16[8,4,768]{2,1,0:T(4,128)(2,1)}, u32[]{:S(2)}) copy-start(bf16[8,4,768]{2,1,0:T(4,128)(2,1)} %param.11) | copy-start | bytes 147460
  52.7 187.3 %all-to-all-start.2 = ((bf16[64,2,32,512]{3,2,1,0:T(8,128)(2,1)}), bf16[64,2,32,512]{3,2,1,0:T(8,128)(2,1)}, u32[]{:S(2)}, u32[]{:S(2)}) async-start(bf16[64,2,32,512]{3,2,1,0:T(8,128)(2,1)} %broadcast_select_fusion), calls=%async_computation.2 | async-start | bytes 8388608 | tf_op jit(solution)/shard_map/all_to_all | solution.py:36
  58.5 243.8 %all-gather.2.cloned.1.call-start = ((), (), s32[]{:S(2)}) async-start(), calls=%async_computation.4 | async-start | bytes 4718592 | tf_op jit(solution)/shard_map/all_gather | solution.py:45
  243.8 20.6 %copy-start.2 = (bf16[1,768]{1,0:T(2,128)(2,1)S(1)}, bf16[1,768]{1,0:T(2,128)(2,1)}, u32[]{:S(2)}) copy-start(bf16[1,768]{1,0:T(2,128)(2,1)} %param.8) | copy-start | bytes 4612
  246.4 53.8 %all-to-all-start.1 = ((bf16[64,2,4,768]{3,2,1,0:T(4,128)(2,1)}), bf16[64,2,4,768]{3,2,1,0:T(4,128)(2,1)}, u32[]{:S(2)}, u32[]{:S(2)}) async-start(bf16[64,2,4,768]{3,2,1,0:T(4,128)(2,1)} %broadcast_select_fusion.1), calls=%async_computation.1 | async-start | bytes 1572864 | tf_op jit(solution)/shard_map/all_to_all | solution.py:38
  336.8 28.8 %all-to-all-start.3 = ((f32[64,2,768]{2,1,0:T(2,128)}), f32[64,2,768]{2,1,0:T(2,128)S(1)}, u32[]{:S(2)}, u32[]{:S(2)}) async-start(f32[64,2,768]{2,1,0:T(2,128)} %reshape.251), calls=%async_computation.3 | async-start | bytes 786432 | tf_op jit(solution)/shard_map/all_to_all | solution.py:69
Sparse Core Ops, SparseCore 0:
  243.9 39.9 all-gather.1
where the time goes:
time: 380 us; the launch traced here: 374 us
  waiting for transfers between devices  238 us (63%)
  blocking collectives  57.1 us (15%)
  starting transfers between devices  27.7 us (7%)
  local copies, waits for them, and re-layouts  16.5 us (4%)
  between operations  14.2 us (4%)
  other arithmetic  14.1 us (4%)
  matrix products  6.57 us (2%)
    all_to_all x1, waiting for transfers between devices, body(): lax.all_to_all(states, 'dp', split_axis=0, concat_axis=0, tiled=True)  181 us
    all_to_all x1, waiting for transfers between devices, body(): lax.all_to_all(tokens, 'dp', split_axis=0, concat_axis=0, tiled=True)  35.9 us
    all_to_all x1, blocking collectives, body(): lax.all_to_all(requests, 'dp', split_axis=0, concat_axis=0, tiled=True)  32.4 us
    psum x1, blocking collectives, body(): mass, pooled = lax.psum((mass_part, pooled_part), 'mp')  24.7 us
    all_to_all x1, waiting for transfers between devices, body(): lax.all_to_all(outgoing.reshape(shards, CAP, retr_width), 'dp', split_axi...  20.1 us
    all_to_all x1, starting transfers between devices, body(): lax.all_to_all(tokens, 'dp', split_axis=0, concat_axis=0, tiled=True)  14.1 us
    all_to_all x1, starting transfers between devices, body(): lax.all_to_all(outgoing.reshape(shards, CAP, retr_width), 'dp', split_axi...  7.81 us
  transfers between devices with their start and end apart: 4, of which 3 were waited for; matrix products, arithmetic and copies ran while one was open for 3% of the time, Pallas kernels for 0%

commit v1 on v0

v1 whole, which is shorter than its diff:
```python
import functools

import jax
import jax.numpy as jnp
from jax import lax
from jax.experimental import pallas as pl
from jax.experimental.pallas import tpu as pltpu
from jax.sharding import PartitionSpec as P

HD = 64
MESH = pl.DeviceIdType.MESH
HIGH = lax.Precision.HIGHEST
NEG = -3e38
F32 = jnp.float32
BF16 = jnp.bfloat16
NT = (((1,), (1,)), ((), ()))
CHUNKS = 4
Y = 4
X = 4


def dot(a, b):
    return jnp.dot(a, b, preferred_element_type=F32)


def dot_nt(a, b):
    return lax.dot_general(a, b, NT, preferred_element_type=F32)


def split3(a):
    first = a.astype(BF16)
    rest = a - first.astype(F32)
    second = rest.astype(BF16)
    third = (rest - second.astype(F32)).astype(BF16)
    return first, second, third


def kernel(
    Z, length, total_heads,
    picks, qe, dec, states, retr, kw, rw,
    ge_out, gq_out,
    st, wb, wrb, gb, ym, pp, pr, pg, bt, qx, q8, c4, cm, em, r4, ob, lz, yb, mb, dz, dt, gs, gyr,
    load_sem, st_s, st_r, gz_s, gz_r, gy_s, gy_r, ym_s, ym_r, pr_s, pr_r, pg_s, pg_r, pc_s, pc_r,
    lz_s, lz_r, yb_s, yb_r, mb_s, mb_r, dz_s, dz_r, qy_s, qy_r,
):
    d = lax.axis_index("dp")
    m = lax.axis_index("mp")
    y, z = d // Z, lax.rem(d, Z)
    x, c = m // 2, lax.rem(m, 2)
    M8 = 2 * X
    other = 1 - c
    xl, xr, xo = lax.rem(x + X - 1, X), lax.rem(x + 1, X), lax.rem(x + 2, X)
    mL, mR, mO, sib = xl * 2 + c, xr * 2 + c, xo * 2 + c, x * 2 + other
    sL, sR, sO = xl * 2 + other, xr * 2 + other, xo * 2 + other
    width = states.shape[1]
    rows = states.shape[0]
    step = rows // CHUNKS
    answers = dec.shape[0]
    p_dev = rows // length
    dr = qe.shape[1]
    nb = dr // 128
    half = nb // 2

    load_st = pltpu.make_async_copy(states, st.at[m], load_sem.at[0])
    load_w = pltpu.make_async_copy(kw, wb, load_sem.at[1])
    load_r = pltpu.make_async_copy(rw, wrb, load_sem.at[2])
    load_st.start()
    load_w.start()
    load_r.start()

    barrier = pltpu.get_barrier_semaphore()

    def hello(i, carry):
        zt = lax.rem(z + i, Z)
        pl.semaphore_signal(barrier, inc=1, device_id=(y * Z + zt, m), device_id_type=MESH)
        return carry

    lax.fori_loop(1, Z, hello, 0)
    for i in range(1, Y):
        pl.semaphore_signal(barrier, inc=1, device_id=(lax.rem(y + i, Y) * Z + z, m), device_id_type=MESH)
    for i in range(1, M8):
        pl.semaphore_signal(barrier, inc=1, device_id=(d, lax.rem(m + i, M8)), device_id_type=MESH)

    part = jnp.sum(retr[...].astype(F32), axis=1)
    for h in range(2):
        for j in range(half):
            b = h * half + j
            pp[h, j * p_dev:(j + 1) * p_dev, :] = part[:, b * 128:(b + 1) * 128]

    ident = lax.broadcasted_iota(jnp.int32, (8, 128), 0) * 128 + lax.broadcasted_iota(jnp.int32, (8, 128), 1)
    counts = jnp.zeros((8, 128), F32)
    for k in range(picks.shape[1]):
        counts = counts + jnp.where(ident == picks[0, k], 1.0, 0.0)
    ym[y, 0:8, :] = jnp.zeros((8, 128), F32)
    qf = qe[...].astype(F32)
    for j in range(nb):
        ym[y, j:j + 1, :] = qf[:, j * 128:(j + 1) * 128]
    ym[y, 8:16, :] = counts

    mine = dec[:, pl.ds(pl.multiple_of(m * 256, 256), 256)].astype(F32)
    block = jnp.concatenate(
        [mine[:, :128], mine[:, 128:], ym[y, 0:8, :], jnp.zeros((8, 128), F32)], axis=0
    )
    gb[y, z] = block.astype(BF16)

    load_st.wait()
    pl.semaphore_wait(barrier, Z - 1 + Y - 1 + M8 - 1)

    def pool_copy(i):
        to = lax.rem(m + i, M8)
        return pltpu.make_async_remote_copy(
            pp.at[lax.rem(to, 2)], pr.at[m], pr_s.at[i], pr_r.at[m], device_id=(d, to), device_id_type=MESH
        )

    def pool_from(i):
        src = lax.rem(m + i, M8)
        return pltpu.make_async_remote_copy(
            pp.at[0], pr.at[src], pr_s.at[0], pr_r.at[src], device_id=(d, sib), device_id_type=MESH
        )

    def block_copy(src, j, to, k):
        at = st.at[src, pl.ds(j * step, step), :]
        return pltpu.make_async_remote_copy(
            at, at, st_s.at[k], st_r.at[src, j], device_id=(d, to), device_id_type=MESH
        )

    def gz_copy(i):
        zt = lax.rem(z + i, Z)
        return pltpu.make_async_remote_copy(
            gb.at[y, z], gb.at[y, z], gz_s.at[i], gz_r.at[z], device_id=(y * Z + zt, m), device_id_type=MESH
        )

    def gz_from(i):
        src = lax.rem(z + i, Z)
        return pltpu.make_async_remote_copy(
            gb.at[y, src], gb.at[y, src], gz_s.at[0], gz_r.at[src], device_id=(y * Z + src, m), device_id_type=MESH
        )

    def y_copy(buf, ssem, rsem, i):
        to = lax.rem(y + i, Y) * Z + z
        return pltpu.make_async_remote_copy(
            buf.at[y], buf.at[y], ssem.at[i], rsem.at[y], device_id=(to, m), device_id_type=MESH
        )

    def y_from(buf, ssem, rsem, i):
        src = lax.rem(y + i, Y)
        return pltpu.make_async_remote_copy(
            buf.at[src], buf.at[src], ssem.at[0], rsem.at[src], device_id=(src * Z + z, m), device_id_type=MESH
        )

    def pg_copy(i):
        zt = lax.rem(z + i, Z)
        return pltpu.make_async_remote_copy(
            pg.at[c, z], pg.at[c, z], pg_s.at[i], pg_r.at[z], device_id=(y * Z + zt, m), device_id_type=MESH
        )

    def pg_from(i):
        src = lax.rem(z + i, Z)
        return pltpu.make_async_remote_copy(
            pg.at[c, src], pg.at[c, src], pg_s.at[0], pg_r.at[src], device_id=(y * Z + src, m), device_id_type=MESH
        )

    def loop(make, act):
        def one(i, carry):
            getattr(make(i), act)()
            return carry

        lax.fori_loop(1, Z, one, 0)

    sent = []

    def push(src, j, to):
        copy = block_copy(src, j, to, len(sent))
        copy.start()
        sent.append(copy)

    def arrived(src, j):
        block_copy(src, j, sib, 0).wait_recv()

    for i in range(1, M8):
        pool_copy(i).start()
    for i in range(CHUNKS):
        push(m, i, mR)
        push(m, (i + CHUNKS // 2) % CHUNKS, mL)
        push(m, i, sib)
    loop(gz_copy, "start")
    for i in range(1, Y):
        y_copy(ym, ym_s, ym_r, i).start()

    load_w.wait()

    def product(src):
        return dot(st[src], wb[pl.ds(pl.multiple_of(src * width, width), width), :])

    keys = product(m)

    for i in range(1, M8):
        pool_from(i).wait_recv()
    pooled = pp[c]
    for i in range(1, M8):
        pooled = pooled + pr[lax.rem(m + i, M8)]
    pooled = pooled / length
    pg[c, z] = jnp.concatenate([pooled, jnp.zeros((32 - half * p_dev, 128), F32)], axis=0).astype(BF16)
    loop(pg_copy, "start")

    h2 = CHUNKS // 2
    for j in range(h2):
        arrived(mL, j)
        push(mL, j, mR)
        push(mL, j, sib)
        arrived(mR, j + h2)
        push(mR, j + h2, mL)
        push(mR, j + h2, sib)

    for i in range(1, Y):
        y_from(ym, ym_s, ym_r, i).wait_recv()
    q8[...] = jnp.zeros_like(q8)
    c4[...] = jnp.zeros_like(c4)
    for i in range(Y):
        c4[i:i + 1, :] = ym[i, pl.ds(8 + y, 1), :]
        for j in range(nb):
            q8[i:i + 1, j * 128:(j + 1) * 128] = ym[i, j:j + 1, :]
    spread = jnp.concatenate(
        [jnp.broadcast_to(c4[i:i + 1, :], (answers, 128)) for _ in range(128 // (Y * answers)) for i in range(Y)], axis=0
    )
    cm[...] = spread.T

    for j in range(h2):
        arrived(mL, j + h2)
        push(mL, j + h2, sib)
        arrived(mR, j)
        push(mR, j, sib)
        if j == 0:
            loop(gz_from, "wait_recv")
            for i in range(1, Y):
                y_copy(gb, gy_s, gy_r, i).start()
    for j in range(CHUNKS):
        arrived(sib, j)
    keys = keys + product(mL) + product(mR) + product(sib)

    for j in range(h2):
        arrived(mO, j)
        push(mO, j, sib)
        arrived(mO, j + h2)
        push(mO, j + h2, sib)
    keys = keys + product(mO)

    for i in range(1, Y):
        y_from(gb, gy_s, gy_r, i).wait_recv()
    low = lax.broadcasted_iota(jnp.int32, (8, 128), 1) < HD
    zero = jnp.zeros((8, 128), F32)
    zeros = jnp.zeros((64, 128), F32)

    def spread_queries(s, carry):
        got = [gb[i, s].astype(F32) for i in range(Y)]
        left = [jnp.where(low, g[0:8], zero) for g in got] + [jnp.where(low, zero, g[0:8]) for g in got]
        right = [jnp.where(low, g[8:16], zero) for g in got] + [jnp.where(low, zero, g[8:16]) for g in got]
        left = jnp.concatenate(left + [zeros], axis=0)
        right = jnp.concatenate([zeros] + right, axis=0)
        bt[s] = jnp.concatenate([left, right], axis=1).astype(BF16)
        qx[s] = jnp.zeros((8, dr), F32)
        for i in range(Y):
            for j in range(nb):
                qx[s, i:i + 1, j * 128:(j + 1) * 128] = got[i][16 + j:17 + j, :]
        return carry

    lax.fori_loop(0, Z, spread_queries, 0)

    for src in (sL, sR, sO):
        for j in range(CHUNKS):
            arrived(src, j)
        keys = keys + product(src)

    to_row = lax.broadcasted_iota(jnp.int32, (rows, rows), 0)
    from_row = lax.broadcasted_iota(jnp.int32, (rows, rows), 1)
    perm = jnp.where(
        from_row == lax.rem(to_row, p_dev) * length + to_row // p_dev, 1.0, 0.0
    ).astype(BF16)
    k1, k2, k3 = [dot(perm, k).astype(BF16) for k in split3(keys)]

    def lz_copy(zt, k):
        return pltpu.make_async_remote_copy(
            ob.at[zt], lz.at[z], lz_s.at[k], lz_r.at[z], device_id=(y * Z + zt, m), device_id_type=MESH
        )

    def lz_from(i):
        src = lax.rem(z + i, Z)
        return pltpu.make_async_remote_copy(
            ob.at[src], lz.at[src], lz_s.at[0], lz_r.at[src], device_id=(y * Z + src, m), device_id_type=MESH
        )

    def lse_pair(z0, z1):
        both = jnp.concatenate([bt[z0], bt[z1]], axis=0)
        scores = dot_nt(k1, both) + dot_nt(k2, both) + dot_nt(k3, both)
        scores = scores.reshape(length, p_dev, 256)
        top = jnp.max(scores, axis=0)
        return top + jnp.log(jnp.sum(jnp.exp(scores - top[None]), axis=0))

    def far_near(i):
        return lax.rem(z + Z // 2 + i, Z), lax.rem(z + Z // 2 - 1 - i, Z)

    def score_step(i, carry):
        z0, z1 = far_near(i)
        lse = lse_pair(z0, z1)
        ob[z0] = lse[:, :128]
        ob[z1] = lse[:, 128:]
        lz_copy(z0, 2 * i).start()
        lz_copy(z1, 2 * i + 1).start()
        return carry

    lax.fori_loop(0, Z // 2 - 1, score_step, 0)
    zlast, _ = far_near(Z // 2 - 1)
    lse = lse_pair(zlast, z)
    ob[zlast] = lse[:, :128]
    lz_copy(zlast, Z - 2).start()
    lz[z] = lse[:, 128:]

    loop(pg_from, "wait_recv")
    core_copy = pltpu.make_async_remote_copy(
        pg.at[c], pg.at[c], pc_s, pc_r, device_id=(d, sib), device_id_type=MESH
    )
    core_copy.start()
    load_r.wait()
    pltpu.make_async_remote_copy(
        pg.at[other], pg.at[other], pc_s, pc_r, device_id=(d, sib), device_id_type=MESH
    ).wait_recv()
    embeds = None
    for h in range(2):
        got = pg[h].astype(F32)
        for j in range(half):
            b = h * half + j
            piece = got[:, j * p_dev:(j + 1) * p_dev, :].reshape(Z * p_dev, 128).astype(BF16)
            term = dot(piece, wrb[b * 128:(b + 1) * 128, :])
            embeds = term if embeds is None else embeds + term
    em[...] = embeds
    count4 = c4[...]
    rs = lax.dot_general(q8[...], embeds, NT, precision=HIGH, preferred_element_type=F32)
    rs = jnp.where(count4 > 0, rs, NEG)
    rtop = jnp.max(rs, axis=1, keepdims=True)
    rsum = jnp.sum(count4 * jnp.exp(rs - rtop), axis=1, keepdims=True)
    rlse = rtop + jnp.log(jnp.where(rsum > 0, rsum, 1.0))

    loop(lz_from, "wait_recv")
    count = cm[...]
    own = jnp.where(count > 0, lz[...].reshape(128, 128), NEG)
    top = jnp.max(own, axis=0, keepdims=True)
    total = jnp.sum(count * jnp.exp(own - top), axis=0, keepdims=True)
    alse = top + jnp.log(jnp.where(total > 0, total, 1.0))
    row = lax.broadcasted_iota(jnp.int32, (8, 128), 0)
    yb[y] = jnp.where(row == 4, jnp.broadcast_to(alse, (8, 128)), jnp.broadcast_to(rlse, (8, 128)))
    for i in range(1, Y):
        y_copy(yb, yb_s, yb_r, i).start()
    for i in range(1, Y):
        y_from(yb, yb_s, yb_r, i).wait_recv()
    parts = yb[...]
    top = jnp.max(parts, axis=0)
    whole = top + jnp.log(jnp.sum(jnp.exp(parts - top[None]), axis=0))
    attn = count * jnp.exp(own - whole[4:5, :])
    lane = lax.broadcasted_iota(jnp.int32, (8, 128), 1)
    group = jnp.where(lax.rem(lane // answers, Y) == row, 1.0, 0.0)
    mass = lax.dot_general(group, attn, NT, precision=HIGH, preferred_element_type=F32)
    mb[m] = mass / (answers * total_heads)

    def mb_copy(i):
        return pltpu.make_async_remote_copy(
            mb.at[m], mb.at[m], mb_s.at[i], mb_r.at[m], device_id=(d, lax.rem(m + i, M8)), device_id_type=MESH
        )

    def mb_from(i):
        src = lax.rem(m + i, M8)
        return pltpu.make_async_remote_copy(
            mb.at[src], mb.at[src], mb_s.at[0], mb_r.at[src], device_id=(d, src), device_id_type=MESH
        )

    for i in range(1, M8):
        mb_copy(i).start()
    probs = count4 * jnp.exp(rs - whole)
    for i in range(1, M8):
        mb_from(i).wait_recv()
    delta = probs - jnp.sum(mb[...], axis=0)
    dz[z] = delta

    def dz_copy(i):
        zt = lax.rem(z + i, Z)
        return pltpu.make_async_remote_copy(
            dz.at[z], dz.at[z], dz_s.at[i], dz_r.at[z], device_id=(y * Z + zt, m), device_id_type=MESH
        )

    def dz_from(i):
        src = lax.rem(z + i, Z)
        return pltpu.make_async_remote_copy(
            dz.at[src], dz.at[src], dz_s.at[0], dz_r.at[src], device_id=(y * Z + src, m), device_id_type=MESH
        )

    loop(dz_copy, "start")
    grads = jnp.dot(delta, em[...], precision=HIGH, preferred_element_type=F32)
    for i in range(Y):
        gs[i] = grads[i:i + 1, :]

    def qy_copy(i):
        to = lax.rem(y + i, Y)
        return pltpu.make_async_remote_copy(
            gs.at[to], gyr.at[y], qy_s.at[i], qy_r.at[y], device_id=(to * Z + z, m), device_id_type=MESH
        )

    def qy_from(i):
        src = lax.rem(y + i, Y)
        return pltpu.make_async_remote_copy(
            gs.at[src], gyr.at[src], qy_s.at[0], qy_r.at[src], device_id=(src * Z + z, m), device_id_type=MESH
        )

    for i in range(1, Y):
        qy_copy(i).start()
    gyr[y] = gs[y]
    loop(dz_from, "wait_recv")
    dt[...] = dz[...].reshape(Z * 8, 128).T
    back = dt[pl.ds(pl.multiple_of(z * p_dev, 8), p_dev), :]
    embed_all = qx[...].reshape(Z * 8, dr).astype(BF16)
    b1, b2, b3 = split3(back)
    ge_out[...] = dot(b1, embed_all) + dot(b2, embed_all) + dot(b3, embed_all)
    for i in range(1, Y):
        qy_from(i).wait_recv()
    gq_out[...] = gyr[0] + gyr[1] + gyr[2] + gyr[3]

    for copy in sent:
        copy.wait_send()
    for i in range(1, M8):
        pool_copy(i).wait_send()
        mb_copy(i).wait_send()
    for i in range(1, Y):
        y_copy(ym, ym_s, ym_r, i).wait_send()
        y_copy(gb, gy_s, gy_r, i).wait_send()
        y_copy(yb, yb_s, yb_r, i).wait_send()
        qy_copy(i).wait_send()
    core_copy.wait_send()

    def sent_one(i, carry):
        gz_copy(i).wait_send()
        pg_copy(i).wait_send()
        dz_copy(i).wait_send()
        lz_copy(0, i - 1).wait_send()
        return carry

    lax.fori_loop(1, Z, sent_one, 0)


def body(picks, query_embed, dec_queries, passage_states, retr_states, key_weight, retr_weight):
    dp = lax.axis_size("dp")
    mp = lax.axis_size("mp")
    Z = dp // Y
    p_dev, length, width = passage_states.shape
    answers, all_cols = dec_queries.shape[1:]
    dr = retr_weight.shape[0]
    rows = p_dev * length
    states = passage_states.reshape(rows, width)
    dec = dec_queries.reshape(answers, all_cols)
    half_rows = (dr // 256) * p_dev
    dma = pltpu.SemaphoreType.DMA
    vmem = pl.BlockSpec(memory_space=pltpu.VMEM)
    hbm = pl.BlockSpec(memory_space=pl.ANY)
    ge, gq = pl.pallas_call(
        functools.partial(kernel, Z, length, all_cols // HD),
        out_shape=(
            jax.ShapeDtypeStruct((p_dev, dr), F32),
            jax.ShapeDtypeStruct((1, dr), F32),
        ),
        in_specs=[pl.BlockSpec(memory_space=pltpu.SMEM), vmem, vmem, hbm, vmem, hbm, hbm],
        out_specs=(vmem, vmem),
        scratch_shapes=[
            pltpu.VMEM((mp, rows, width), BF16),
            pltpu.VMEM(key_weight.shape, BF16),
            pltpu.VMEM((dr, dr), BF16),
            pltpu.VMEM((Y, Z, 32, 128), BF16),
            pltpu.VMEM((Y, 16, 128), F32),
            pltpu.VMEM((2, half_rows, 128), F32),
            pltpu.VMEM((mp, half_rows, 128), F32),
            pltpu.VMEM((2, Z, 32, 128), BF16),
            pltpu.VMEM((Z, 128, 256), BF16),
            pltpu.VMEM((Z, 8, dr), F32),
            pltpu.VMEM((8, dr), F32),
            pltpu.VMEM((8, 128), F32),
            pltpu.VMEM((128, 128), F32),
            pltpu.VMEM((128, dr), F32),
            pltpu.VMEM((8, 128), F32),
            pltpu.VMEM((Z, 8, 128), F32),
            pltpu.VMEM((Z, 8, 128), F32),
            pltpu.VMEM((Y, 8, 128), F32),
            pltpu.VMEM((mp, 8, 128), F32),
            pltpu.VMEM((Z, 8, 128), F32),
            pltpu.VMEM((128, 128), F32),
            pltpu.VMEM((Y, 1, dr), F32),
            pltpu.VMEM((Y, 1, dr), F32),
            dma((3,)),
            dma((28,)), dma((mp, CHUNKS)),
            dma((Z,)), dma((Z,)),
            dma((Y,)), dma((Y,)),
            dma((Y,)), dma((Y,)),
            dma((mp,)), dma((mp,)),
            dma((Z,)), dma((Z,)),
            dma, dma,
            dma((Z,)), dma((Z,)),
            dma((Y,)), dma((Y,)),
            dma((mp,)), dma((mp,)),
            dma((Z,)), dma((Z,)),
            dma((Y,)), dma((Y,)),
        ],
        compiler_params=pltpu.CompilerParams(
            collective_id=0, has_side_effects=True, vmem_limit_bytes=40 * 1024 * 1024
        ),
    )(picks, query_embed, dec, states, retr_states, key_weight, retr_weight)
    return ge, gq


def solution(mesh):
    placed = (
        P("dp", None),
        P("dp", None),
        P("dp", None, None),
        P("dp", None, "mp"),
        P("dp", "mp", None),
        P(None, "mp"),
        P(),
    )
    return jax.shard_map(
        body, mesh=mesh, in_specs=placed, out_specs=(P("dp", None), P("dp", None)), check_vma=False
    )
```

time: 380 us -> 69.2 us (0.18); the launches traced: 374 us -> 68.8 us
  waiting for transfers between devices: 238 us -> 0 us
  Pallas kernels: 0 us -> 60.3 us
  blocking collectives: 57.1 us -> 0 us
  starting transfers between devices: 27.7 us -> 0 us
  other arithmetic: 14.1 us -> 0 us
  between operations: 14.2 us -> 0.66 us
  local copies, waits for them, and re-layouts: 16.5 us -> 7.89 us
  matrix products: 6.57 us -> 0 us
    all_to_all x3 -> x0, waiting for transfers between devices: 237 us -> none  [the longest x1 181 us: body(): lax.all_to_all(states, 'dp', split_axis=0, concat_axis=0, tiled=True)]
    pallas_call x0 -> x1, Pallas kernels: none -> 60.3 us  [body(): pl.pallas_call(functools.partial(kernel, Z, length, all_cols // HD), out_...]
    all_to_all x1 -> x0, blocking collectives: 32.4 us -> none  [body(): lax.all_to_all(requests, 'dp', split_axis=0, concat_axis=0, tiled=True)]
    all_to_all x3 -> x0, starting transfers between devices: 27.7 us -> none  [the longest x1 14.1 us: body(): lax.all_to_all(tokens, 'dp', split_axis=0, concat_axis=0, tiled=True)]
    psum x1 -> x0, blocking collectives: 24.7 us -> none  [body(): mass, pooled = lax.psum((mass_part, pooled_part), 'mp')]
    gather x4 -> x0, local copies, waits for them, and re-layouts: 9.57 us -> none  [the longest x1 3.74 us: body(): states = jnp.take(passage_states, wanted, axis=0)]
    select_n x4 -> x0, other arithmetic: 7.54 us -> none  [the longest x1 4.56 us: body(): states = jnp.take(passage_states, wanted, axis=0)]
    dot_general x6 -> x0, matrix products: 6.57 us -> none  [the longest x1 3.47 us: body(): keys = jnp.dot(flat_piece, key_weight, preferred_element_type=jnp.float32)]
  transfers between devices with their start and end apart: 4 -> 0, of which waited for: 3 -> 0; matrix products, arithmetic and copies ran while one was open for 3% -> 0% of each run, Pallas kernels for 0% -> 0%
where the time goes in v1:
time: 69.2 us; the launch traced here: 68.8 us
  Pallas kernels  60.3 us (87%)
  local copies, waits for them, and re-layouts  7.89 us (11%)
    pallas_call x1, Pallas kernels, body(): pl.pallas_call(functools.partial(kernel, Z, length, all_cols // HD), out_...  60.3 us
    unnamed x16, local copies, waits for them, and re-layouts  7.89 us

profile of v1, /device:TPU:1, one launch (start us, length us, event | category | flops | bytes accessed | tf_op | source)
XLA Modules:
  0.0 68.8 jit_solution(6411853460015117808)
XLA Ops:
  0.6 0.0 copy-start
  0.6 1.6 %copy-done = bf16[4096,256]{1,0:T(8,128)(2,1)S(1)} copy-done((bf16[4096,256]{1,0:T(8,128)(2,1)S(1)}, bf16[4096,256]{1,0:T(8,128)(2,1)}, u32[]{:S(2)}) %copy-start) | copy-done | bytes 2097176
  2.2 0.0 copy-start.1
  2.2 1.3 %copy-done.1 = bf16[768,768]{1,0:T(8,128)(2,1)S(1)} copy-done((bf16[768,768]{1,0:T(8,128)(2,1)S(1)}, bf16[768,768]{1,0:T(8,128)(2,1)}, u32[]{:S(2)}) %copy-start.1) | copy-done | bytes 1179672
  3.5 0.0 copy-start.2
  3.5 0.9 %copy-done.2 = bf16[8,32,512]{2,1,0:T(8,128)(2,1)S(1)} copy-done((bf16[8,32,512]{2,1,0:T(8,128)(2,1)S(1)}, bf16[8,32,512]{2,1,0:T(8,128)(2,1)}, u32[]{:S(2)}) %copy-start.2) | copy-done | bytes 262168
  4.4 0.0 copy-start.3
  4.4 0.8 %copy-done.3 = bf16[8,4,768]{2,1,0:T(4,128)(2,1)S(1)} copy-done((bf16[8,4,768]{2,1,0:T(4,128)(2,1)S(1)}, bf16[8,4,768]{2,1,0:T(4,128)(2,1)}, u32[]{:S(2)}) %copy-start.3) | copy-done | bytes 49176
  5.2 0.0 copy-start.4
  5.2 0.8 %copy-done.4 = bf16[1,8,2048]{2,1,0:T(8,128)(2,1)S(1)} copy-done((bf16[1,8,2048]{2,1,0:T(8,128)(2,1)S(1)}, bf16[1,8,2048]{2,1,0:T(8,128)(2,1)}, u32[]{:S(2)}) %copy-start.4) | copy-done | bytes 32792
  6.0 0.0 copy-start.5
  6.0 0.7 copy-done.5
  6.7 0.0 copy-start.6
  6.7 0.7 copy-done.6
  7.3 60.3 %shard_map.86 = (f32[8,768]{1,0:T(8,128)S(1)}, f32[1,768]{1,0:T(1,128)S(1)}) custom-call(s32[1,16]{1,0:T(1,128)S(1)} %copy-done.6, bf16[1,768]{1,0:T(2,128)(2,1)S(1)} %copy-done.5, bf16[8,2048]{1,0:T(8,128)(2,1)S(1)} %bitcast.3, bf16[256,512]{1,0:T(8,128)(2,1)S(1)} %bitcast.2, bf16[8,4,768]{2,1,0:T(4,128)(2,1)S(1)} %copy-done.3, ...), custom_call_target="tpu_custom_call" | custom-call | tf_op jit(solution)/shard_map/pallas_call | solution.py:461
  67.7 0.6 copy.11
  68.3 0.6 copy.12
Async XLA Ops:
  0.6 1.6 %copy-start = (bf16[4096,256]{1,0:T(8,128)(2,1)S(1)}, bf16[4096,256]{1,0:T(8,128)(2,1)}, u32[]{:S(2)}) copy-start(bf16[4096,256]{1,0:T(8,128)(2,1)} %kw.1) | copy-start | bytes 6291460
  2.2 1.3 %copy-start.1 = (bf16[768,768]{1,0:T(8,128)(2,1)S(1)}, bf16[768,768]{1,0:T(8,128)(2,1)}, u32[]{:S(2)}) copy-start(bf16[768,768]{1,0:T(8,128)(2,1)} %rw.1) | copy-start | bytes 3538948
  3.5 0.9 %copy-start.2 = (bf16[8,32,512]{2,1,0:T(8,128)(2,1)S(1)}, bf16[8,32,512]{2,1,0:T(8,128)(2,1)}, u32[]{:S(2)}) copy-start(bf16[8,32,512]{2,1,0:T(8,128)(2,1)} %param.10) | copy-start | bytes 786436
  4.4 0.8 %copy-start.3 = (bf16[8,4,768]{2,1,0:T(4,128)(2,1)S(1)}, bf16[8,4,768]{2,1,0:T(4,128)(2,1)}, u32[]{:S(2)}) copy-start(bf16[8,4,768]{2,1,0:T(4,128)(2,1)} %retr.1) | copy-start | bytes 147460
  5.2 0.8 %copy-start.4 = (bf16[1,8,2048]{2,1,0:T(8,128)(2,1)S(1)}, bf16[1,8,2048]{2,1,0:T(8,128)(2,1)}, u32[]{:S(2)}) copy-start(bf16[1,8,2048]{2,1,0:T(8,128)(2,1)} %param.9) | copy-start | bytes 98308
  6.0 0.7 copy-start.5
  6.7 0.7 copy-start.6

commit v2 on v1

v2 whole, which is shorter than its diff:
```python
import functools

import jax
import jax.numpy as jnp
from jax import lax
from jax.experimental import pallas as pl
from jax.experimental.pallas import tpu as pltpu
from jax.sharding import PartitionSpec as P

HD = 64
MESH = pl.DeviceIdType.MESH
NEG = -3e38
F32 = jnp.float32
BF16 = jnp.bfloat16
NT = (((1,), (1,)), ((), ()))
CHUNKS = 4
Y = 4
X = 4


def dot(a, b):
    return jnp.dot(a, b, preferred_element_type=F32)


def dot_nt(a, b):
    return lax.dot_general(a, b, NT, preferred_element_type=F32)


def split2(a):
    first = a.astype(BF16)
    return first, (a - first.astype(F32)).astype(BF16)


def kernel(
    Z, length, total_heads,
    picks_hbm, qe_hbm, dec_hbm, states, retr_hbm, kw, rw,
    ge_out, gq_out,
    picks, qe, dec, retr, st, wb, wrb, gb, qb, ym, pp, pr, pg, qx, q8, c4, cm, em, ob, lz, yb, mb, dz, gs, gyr,
    load_sem, st_s, st_r, gz_s, gz_r, gy_s, gy_r, qz_s, qz_r, qw_s, qw_r, ym_s, ym_r, pr_s, pr_r, pg_s, pg_r,
    pc_s, pc_r, lz_s, lz_r, yb_s, yb_r, mb_s, mb_r, dz_s, dz_r, qy_s, qy_r,
):
    d = lax.axis_index("dp")
    m = lax.axis_index("mp")
    y, z = d // Z, lax.rem(d, Z)
    x, c = m // 2, lax.rem(m, 2)
    M8 = 2 * X
    other = 1 - c
    xl, xr, xo = lax.rem(x + X - 1, X), lax.rem(x + 1, X), lax.rem(x + 2, X)
    mL, mR, mO, sib = xl * 2 + c, xr * 2 + c, xo * 2 + c, x * 2 + other
    sL, sR, sO = xl * 2 + other, xr * 2 + other, xo * 2 + other
    rows, width = states.shape
    step = rows // CHUNKS
    answers = dec.shape[0]
    p_dev = rows // length
    dr = qe.shape[1]
    nb = dr // 128
    half = nb // 2

    load_st = pltpu.make_async_copy(states, st.at[m], load_sem.at[0])
    load_w = pltpu.make_async_copy(kw, wb, load_sem.at[1])
    load_r = pltpu.make_async_copy(rw, wrb, load_sem.at[2])
    load_dec = pltpu.make_async_copy(dec_hbm, dec, load_sem.at[3])
    load_qe = pltpu.make_async_copy(qe_hbm, qe, load_sem.at[4])
    load_picks = pltpu.make_async_copy(picks_hbm, picks, load_sem.at[5])
    load_retr = pltpu.make_async_copy(retr_hbm, retr, load_sem.at[6])
    for copy in (load_dec, load_qe, load_picks, load_retr, load_st, load_w, load_r):
        copy.start()

    barrier = pltpu.get_barrier_semaphore()

    def hello(i, carry):
        zt = lax.rem(z + i, Z)
        pl.semaphore_signal(barrier, inc=1, device_id=(y * Z + zt, m), device_id_type=MESH)
        return carry

    lax.fori_loop(1, Z, hello, 0)
    for i in range(1, Y):
        pl.semaphore_signal(barrier, inc=1, device_id=(lax.rem(y + i, Y) * Z + z, m), device_id_type=MESH)
    for i in range(1, M8):
        pl.semaphore_signal(barrier, inc=1, device_id=(d, lax.rem(m + i, M8)), device_id_type=MESH)

    pl.semaphore_wait(barrier, Z - 1 + Y - 1 + M8 - 1)
    def remote(src, dst, ssem, rsem, dev):
        return pltpu.make_async_remote_copy(src, dst, ssem, rsem, device_id=dev, device_id_type=MESH)

    def z_send(buf, ssem, rsem):
        def one(i, carry):
            zt = lax.rem(z + i, Z)
            remote(buf.at[z], buf.at[z], ssem, rsem, (y * Z + zt, m)).start()
            return carry

        lax.fori_loop(1, Z, one, 0)

    def z_all(buf, ssem, rsem):
        at = buf.at[pl.ds(0, Z - 1)]
        return remote(at, at, ssem, rsem, (y * Z + lax.rem(z + 1, Z), m))

    def y_copy(buf, ssem, rsem, i):
        to = lax.rem(y + i, Y) * Z + z
        return remote(buf.at[y], buf.at[y], ssem, rsem, (to, m))

    def y_all(buf, ssem, rsem):
        at = buf.at[pl.ds(0, Y - 1)]
        return remote(at, at, ssem, rsem, (lax.rem(y + 1, Y) * Z + z, m))

    def y_send(buf, ssem, rsem):
        for i in range(1, Y):
            y_copy(buf, ssem, rsem, i).start()

    sent = []

    def push(src, j, to, own=False):
        k = len(sent)
        at = st.at[src, pl.ds(j * step, step), :]
        copy = remote(states.at[pl.ds(j * step, step), :] if own else at, at, st_s.at[k], st_r.at[src, j], (d, to))
        copy.start()
        sent.append(copy)

    def arrived(src, j):
        at = st.at[src, pl.ds(j * step, step), :]
        remote(at, at, st_s.at[0], st_r.at[src, j], (d, sib)).wait_recv()

    gz = gb.at[y]
    h2 = CHUNKS // 2
    for i in range(h2):
        push(m, i, mR, True)
        push(m, i + h2, mL, True)

    load_dec.wait()
    mine = dec[:, pl.ds(pl.multiple_of(m * 256, 256), 256)].astype(F32)
    gb[y, z] = jnp.concatenate([mine[:, :128], mine[:, 128:]], axis=0).astype(BF16)
    z_send(gz, gz_s, gz_r)

    load_retr.wait()
    part = jnp.sum(retr[...].astype(F32), axis=1)
    for h in range(2):
        for j in range(half):
            b = h * half + j
            pp[h, j * p_dev:(j + 1) * p_dev, :] = part[:, b * 128:(b + 1) * 128]

    def pool_copy(i):
        to = lax.rem(m + i, M8)
        return remote(pp.at[lax.rem(to, 2)], pr.at[m], pr_s, pr_r, (d, to))

    for i in range(1, M8):
        pool_copy(i).start()

    for i in range(h2):
        push(m, i + h2, mR, True)
        push(m, i, mL, True)
    for i in range(CHUNKS):
        push(m, i, sib, True)

    load_picks.wait()
    load_qe.wait()
    ident = lax.broadcasted_iota(jnp.int32, (8, 128), 0) * 128 + lax.broadcasted_iota(jnp.int32, (8, 128), 1)
    counts = jnp.zeros((8, 128), F32)
    for k in range(picks.shape[1]):
        counts = counts + jnp.where(ident == picks[0, k], 1.0, 0.0)
    ym[y, 0:8, :] = jnp.zeros((8, 128), F32)
    qf = qe[...].astype(F32)
    for j in range(nb):
        ym[y, j:j + 1, :] = qf[:, j * 128:(j + 1) * 128]
    ym[y, 8:16, :] = counts
    qb[y, z] = ym[y, 0:8, :]
    y_send(ym, ym_s, ym_r)
    z_send(qb.at[y], qz_s, qz_r)

    load_st.wait()
    load_w.wait()

    def product(src):
        return dot(st[src], wb[pl.ds(pl.multiple_of(src * width, width), width), :])

    keys = product(m)

    for j in range(h2):
        arrived(mL, j)
        push(mL, j, mR)
        push(mL, j, sib)
        arrived(mR, j + h2)
        push(mR, j + h2, mL)
        push(mR, j + h2, sib)

    pool_all = remote(pr.at[pl.ds(0, M8 - 1)], pr.at[pl.ds(0, M8 - 1)], pr_s, pr_r, (d, sib))
    pool_all.wait_recv()
    pooled = pp[c]
    for i in range(1, M8):
        pooled = pooled + pr[lax.rem(m + i, M8)]
    pooled = pooled / length
    pg[c, z] = jnp.concatenate([pooled, jnp.zeros((32 - half * p_dev, 128), F32)], axis=0).astype(BF16)
    z_send(pg.at[c], pg_s, pg_r)

    for j in range(h2):
        arrived(mL, j + h2)
        push(mL, j + h2, sib)
        arrived(mR, j)
        push(mR, j, sib)

    z_all(gz, gz_s, gz_r).wait_recv()
    y_send(gb, gy_s, gy_r)

    y_all(ym, ym_s, ym_r).wait_recv()
    q8[...] = jnp.zeros_like(q8)
    c4[...] = jnp.zeros_like(c4)
    for i in range(Y):
        c4[i:i + 1, :] = ym[i, pl.ds(8 + y, 1), :]
        for j in range(nb):
            q8[i:i + 1, j * 128:(j + 1) * 128] = ym[i, j:j + 1, :]
    spread = jnp.concatenate(
        [jnp.broadcast_to(c4[i:i + 1, :], (answers, 128)) for _ in range(128 // (Y * answers)) for i in range(Y)], axis=0
    )
    cm[...] = spread.T

    for j in range(CHUNKS):
        arrived(sib, j)
    keys = keys + product(mL) + product(mR) + product(sib)
    for j in range(h2):
        arrived(mO, j)
        push(mO, j, sib)
        arrived(mO, j + h2)
        push(mO, j + h2, sib)
    keys = keys + product(mO)
    for src in (sL, sR, sO):
        for j in range(CHUNKS):
            arrived(src, j)
        keys = keys + product(src)

    to_row = lax.broadcasted_iota(jnp.int32, (rows, rows), 0)
    from_row = lax.broadcasted_iota(jnp.int32, (rows, rows), 1)
    perm = jnp.where(
        from_row == lax.rem(to_row, p_dev) * length + to_row // p_dev, 1.0, 0.0
    ).astype(BF16)
    k1, k2 = [dot(perm, k).astype(BF16) for k in split2(keys)]

    y_all(gb, gy_s, gy_r).wait_recv()
    low = lax.broadcasted_iota(jnp.int32, (8, 128), 1) < HD
    zero = jnp.zeros((8, 128), F32)
    zeros = jnp.zeros((64, 128), F32)

    def spread_queries(s):
        got = [gb[i, s].astype(F32) for i in range(Y)]
        left = [jnp.where(low, g[0:8], zero) for g in got] + [jnp.where(low, zero, g[0:8]) for g in got]
        right = [jnp.where(low, g[8:16], zero) for g in got] + [jnp.where(low, zero, g[8:16]) for g in got]
        left = jnp.concatenate(left + [zeros], axis=0)
        right = jnp.concatenate([zeros] + right, axis=0)
        return jnp.concatenate([left, right], axis=1).astype(BF16)

    def lz_copy(zt):
        return remote(ob.at[zt], lz.at[z], lz_s, lz_r, (y * Z + zt, m))

    def lse_pair(z0, z1):
        both = jnp.concatenate([spread_queries(z0), spread_queries(z1)], axis=0)
        scores = dot_nt(k1, both) + dot_nt(k2, both)
        scores = scores.reshape(length, p_dev, 256)
        top = jnp.max(scores, axis=0)
        return top + jnp.log(jnp.sum(jnp.exp(scores - top[None]), axis=0))

    def far_near(i):
        return lax.rem(z + Z // 2 + i, Z), lax.rem(z + Z // 2 - 1 - i, Z)

    def score_step(i, carry):
        z0, z1 = far_near(i)
        lse = lse_pair(z0, z1)
        ob[z0] = lse[:, :128]
        ob[z1] = lse[:, 128:]
        lz_copy(z0).start()
        lz_copy(z1).start()
        return carry

    lax.fori_loop(0, Z // 2 - 1, score_step, 0)
    zlast, _ = far_near(Z // 2 - 1)
    lse = lse_pair(zlast, z)
    ob[zlast] = lse[:, :128]
    lz_copy(zlast).start()
    lz[z] = lse[:, 128:]

    z_all(qb.at[y], qz_s, qz_r).wait_recv()
    y_send(qb, qw_s, qw_r)

    pgz = pg.at[c]
    z_all(pgz, pg_s, pg_r).wait_recv()
    core_copy = remote(pg.at[c], pg.at[c], pc_s, pc_r, (d, sib))
    core_copy.start()
    load_r.wait()
    remote(pg.at[other], pg.at[other], pc_s, pc_r, (d, sib)).wait_recv()
    embeds = None
    for h in range(2):
        got = pg[h].astype(F32)
        for j in range(half):
            b = h * half + j
            piece = got[:, j * p_dev:(j + 1) * p_dev, :].reshape(Z * p_dev, 128).astype(BF16)
            term = dot(piece, wrb[b * 128:(b + 1) * 128, :])
            embeds = term if embeds is None else embeds + term
    e1, e2 = split2(embeds)
    em[0] = e1
    em[1] = e2
    count4 = c4[...]
    q1 = q8[...].astype(BF16)
    rs = dot_nt(q1, e1) + dot_nt(q1, e2) + dot_nt(q1, (embeds - e1.astype(F32) - e2.astype(F32)).astype(BF16))
    rs = jnp.where(count4 > 0, rs, NEG)
    rtop = jnp.max(rs, axis=1, keepdims=True)
    rsum = jnp.sum(count4 * jnp.exp(rs - rtop), axis=1, keepdims=True)
    rlse = rtop + jnp.log(jnp.where(rsum > 0, rsum, 1.0))

    for copy in sent:
        copy.wait_send()
    pool_all.wait_send()
    z_all(gz, gz_s, gz_r).wait_send()
    z_all(qb.at[y], qz_s, qz_r).wait_send()
    y_all(ym, ym_s, ym_r).wait_send()
    y_all(gb, gy_s, gy_r).wait_send()

    z_all(lz, lz_s, lz_r).wait_recv()
    count = cm[...]
    own = jnp.where(count > 0, lz[...].reshape(128, 128), NEG)
    top = jnp.max(own, axis=0, keepdims=True)
    weight = count * jnp.exp(own - top)
    total = jnp.sum(weight, axis=0, keepdims=True)
    alse = top + jnp.log(jnp.where(total > 0, total, 1.0))
    row = lax.broadcasted_iota(jnp.int32, (8, 128), 0)
    yb[y] = jnp.where(row == 4, jnp.broadcast_to(alse, (8, 128)), jnp.broadcast_to(rlse, (8, 128)))
    y_send(yb, yb_s, yb_r)
    w1, w2 = split2(weight)
    lane = lax.broadcasted_iota(jnp.int32, (8, 128), 1)
    group = jnp.where(lax.rem(lane // answers, Y) == row, 1.0 / (answers * total_heads), 0.0)
    z_all(lz, lz_s, lz_r).wait_send()
    z_all(pgz, pg_s, pg_r).wait_send()
    core_copy.wait_send()
    y_all(qb, qw_s, qw_r).wait()
    y_all(yb, yb_s, yb_r).wait_recv()
    parts = yb[...]
    ptop = jnp.max(parts, axis=0)
    whole = ptop + jnp.log(jnp.sum(jnp.exp(parts - ptop[None]), axis=0))
    g1, g2 = split2(group * jnp.exp(top - whole[4:5, :]))
    mb[m] = dot_nt(g1, w1) + dot_nt(g1, w2) + dot_nt(g2, w1)

    def mb_copy(i):
        return remote(mb.at[m], mb.at[m], mb_s, mb_r, (d, lax.rem(m + i, M8)))

    mb_all = remote(mb.at[pl.ds(0, M8 - 1)], mb.at[pl.ds(0, M8 - 1)], mb_s, mb_r, (d, sib))
    for i in range(1, M8):
        mb_copy(i).start()
    probs = count4 * jnp.exp(rs - whole)

    def spread_embed(s, carry):
        qx[s] = jnp.zeros((8, dr), F32)
        for i in range(Y):
            for j in range(nb):
                qx[s, i:i + 1, j * 128:(j + 1) * 128] = qb[i, s, j:j + 1, :]
        return carry

    lax.fori_loop(0, Z, spread_embed, 0)
    embed_all = qx[...].reshape(Z * 8, dr).astype(BF16)
    mine_only = jnp.where(lane == row + z * p_dev, 1.0, 0.0).astype(BF16)
    y_all(yb, yb_s, yb_r).wait_send()
    mb_all.wait_recv()
    delta = probs - jnp.sum(mb[...], axis=0)
    dz[z] = delta
    z_send(dz, dz_s, dz_r)
    d1, d2 = split2(delta)
    grads = dot(d1, em[0]) + dot(d1, em[1]) + dot(d2, em[0])
    for i in range(Y):
        gs[i] = grads[i:i + 1, :]

    def qy_copy(i):
        to = lax.rem(y + i, Y)
        return remote(gs.at[to], gyr.at[y], qy_s, qy_r, (to * Z + z, m))

    for i in range(1, Y):
        qy_copy(i).start()
    gyr[y] = gs[y]
    mb_all.wait_send()
    y_all(gyr, qy_s, qy_r).wait()
    gq_out[...] = gyr[0] + gyr[1] + gyr[2] + gyr[3]
    z_all(dz, dz_s, dz_r).wait()
    b1, b2 = [dot_nt(mine_only, part).astype(BF16) for part in split2(dz[...].reshape(Z * 8, 128))]
    ge_out[...] = dot(b1, embed_all) + dot(b2, embed_all)


def body(picks, query_embed, dec_queries, passage_states, retr_states, key_weight, retr_weight):
    dp = lax.axis_size("dp")
    mp = lax.axis_size("mp")
    Z = dp // Y
    p_dev, length, width = passage_states.shape
    answers, all_cols = dec_queries.shape[1:]
    dr = retr_weight.shape[0]
    rows = p_dev * length
    states = passage_states.reshape(rows, width)
    dec = dec_queries.reshape(answers, all_cols)
    half_rows = (dr // 256) * p_dev
    dma = pltpu.SemaphoreType.DMA
    vmem = pl.BlockSpec(memory_space=pltpu.VMEM)
    hbm = pl.BlockSpec(memory_space=pltpu.HBM)
    ge, gq = pl.pallas_call(
        functools.partial(kernel, Z, length, all_cols // HD),
        out_shape=(
            jax.ShapeDtypeStruct((p_dev, dr), F32),
            jax.ShapeDtypeStruct((1, dr), F32),
        ),
        in_specs=[hbm] * 7,
        out_specs=(vmem, vmem),
        scratch_shapes=[
            pltpu.SMEM(picks.shape, jnp.int32),
            pltpu.VMEM(query_embed.shape, BF16),
            pltpu.VMEM(dec.shape, BF16),
            pltpu.VMEM(retr_states.shape, BF16),
            pltpu.VMEM((mp, rows, width), BF16),
            pltpu.VMEM(key_weight.shape, BF16),
            pltpu.VMEM((dr, dr), BF16),
            pltpu.VMEM((Y, Z, 16, 128), BF16),
            pltpu.VMEM((Y, Z, 8, 128), F32),
            pltpu.VMEM((Y, 16, 128), F32),
            pltpu.VMEM((2, half_rows, 128), F32),
            pltpu.VMEM((mp, half_rows, 128), F32),
            pltpu.VMEM((2, Z, 32, 128), BF16),
            pltpu.VMEM((Z, 8, dr), F32),
            pltpu.VMEM((8, dr), F32),
            pltpu.VMEM((8, 128), F32),
            pltpu.VMEM((128, 128), F32),
            pltpu.VMEM((2, 128, dr), BF16),
            pltpu.VMEM((Z, 8, 128), F32),
            pltpu.VMEM((Z, 8, 128), F32),
            pltpu.VMEM((Y, 8, 128), F32),
            pltpu.VMEM((mp, 8, 128), F32),
            pltpu.VMEM((Z, 8, 128), F32),
            pltpu.VMEM((Y, 1, dr), F32),
            pltpu.VMEM((Y, 1, dr), F32),
            dma((7,)),
            dma((28,)), dma((mp, CHUNKS)),
            *[dma] * 26,
        ],
        compiler_params=pltpu.CompilerParams(
            collective_id=0, has_side_effects=True, vmem_limit_bytes=63 * 1024 * 1024
        ),
    )(picks, query_embed, dec, states, retr_states, key_weight, retr_weight)
    return ge, gq


def solution(mesh):
    placed = (
        P("dp", None),
        P("dp", None),
        P("dp", None, None),
        P("dp", None, "mp"),
        P("dp", "mp", None),
        P(None, "mp"),
        P(),
    )
    return jax.shard_map(
        body, mesh=mesh, in_specs=placed, out_specs=(P("dp", None), P("dp", None)), check_vma=False
    )
```

time: 69.2 us -> 58.8 us (0.85)
  Pallas kernels: 60.3 us -> 54.9 us
  local copies, waits for them, and re-layouts: 7.89 us -> 2.6 us
    pallas_call x1, Pallas kernels: 60.3 us -> 54.9 us  [body(): pl.pallas_call(functools.partial(kernel, Z, length, all_cols // HD), out_...]
    unnamed x16 -> x2, local copies, waits for them, and re-layouts: 7.89 us -> 2.6 us
where the time goes in v2:
time: 58.8 us; the launch traced here: 58.2 us
  Pallas kernels  54.9 us (93%)
  local copies, waits for them, and re-layouts  2.6 us (4%)
  between operations  0.64 us (1%)
    pallas_call x1, Pallas kernels, body(): pl.pallas_call(functools.partial(kernel, Z, length, all_cols // HD), out_...  54.9 us
    unnamed x2, local copies, waits for them, and re-layouts  2.6 us

profile of v2, /device:TPU:1, one launch (start us, length us, event | category | flops | bytes accessed | tf_op | source)
XLA Modules:
  0.0 58.2 jit_solution(7117435381942247982)
XLA Ops:
  0.6 54.9 %shard_map.86 = (f32[8,768]{1,0:T(8,128)}, f32[1,768]{1,0:T(1,128)}) custom-call(s32[1,16]{1,0:T(1,128)} %picks_hbm.1, bf16[1,768]{1,0:T(2,128)(2,1)} %qe_hbm.1, bf16[8,2048]{1,0:T(8,128)(2,1)} %bitcast.3, bf16[256,512]{1,0:T(8,128)(2,1)} %bitcast.2, bf16[8,4,768]{2,1,0:T(4,128)(2,1)} %retr_hbm.1, bf16[4096,256]{1,0:T(8,128)(2,1)} %kw.1, bf16[768,768]{1,0:T(8,128)(2,1)} %rw.1), custom_call_target="tpu_custom_call" | custom-call | tf_op jit(solution)/shard_map/pallas_call | solution.py:395
  55.6 1.3 %copy.11 = f32[8,768]{1,0:T(8,128)} copy(f32[8,768]{1,0:T(8,128)} %get-tuple-element.4) | data formatting | bytes 49152
  56.9 1.3 %copy.12 = f32[1,768]{1,0:T(1,128)} copy(f32[1,768]{1,0:T(1,128)} %get-tuple-element.5) | data formatting | bytes 6144

commit v3 on v2

--- a/solution.py
+++ b/solution.py
@@ -35,7 +35,7 @@
     Z, length, total_heads,
     picks_hbm, qe_hbm, dec_hbm, states, retr_hbm, kw, rw,
     ge_out, gq_out,
-    picks, qe, dec, retr, st, wb, wrb, gb, qb, ym, pp, pr, pg, qx, q8, c4, cm, em, ob, lz, yb, mb, dz, gs, gyr,
+    picks, qe, dec, retr, st, wb, wrb, gb, qb, ym, pp, pr, pg, qx, q8, c4, cm, em, ob, lz, yb, mb, dz, dp_all, gs, gyr,
     load_sem, st_s, st_r, gz_s, gz_r, gy_s, gy_r, qz_s, qz_r, qw_s, qw_r, ym_s, ym_r, pr_s, pr_r, pg_s, pg_r,
     pc_s, pc_r, lz_s, lz_r, yb_s, yb_r, mb_s, mb_r, dz_s, dz_r, qy_s, qy_r,
 ):
@@ -68,12 +68,19 @@
 
     barrier = pltpu.get_barrier_semaphore()
 
-    def hello(i, carry):
-        zt = lax.rem(z + i, Z)
+    def far_first(act):
+        def two(i, carry):
+            act(lax.rem(z + Z // 2 + i, Z))
+            act(lax.rem(z + Z // 2 - 1 - i, Z))
+            return carry
+
+        lax.fori_loop(0, Z // 2 - 1, two, 0)
+        act(lax.rem(z + Z - 1, Z))
+
+    def hello(zt):
         pl.semaphore_signal(barrier, inc=1, device_id=(y * Z + zt, m), device_id_type=MESH)
-        return carry
-
-    lax.fori_loop(1, Z, hello, 0)
+
+    far_first(hello)
     for i in range(1, Y):
         pl.semaphore_signal(barrier, inc=1, device_id=(lax.rem(y + i, Y) * Z + z, m), device_id_type=MESH)
     for i in range(1, M8):
@@ -84,12 +91,7 @@
         return pltpu.make_async_remote_copy(src, dst, ssem, rsem, device_id=dev, device_id_type=MESH)
 
     def z_send(buf, ssem, rsem):
-        def one(i, carry):
-            zt = lax.rem(z + i, Z)
-            remote(buf.at[z], buf.at[z], ssem, rsem, (y * Z + zt, m)).start()
-            return carry
-
-        lax.fori_loop(1, Z, one, 0)
+        far_first(lambda zt: remote(buf.at[z], buf.at[z], ssem, rsem, (y * Z + zt, m)).start())
 
     def z_all(buf, ssem, rsem):
         at = buf.at[pl.ds(0, Z - 1)]
@@ -150,6 +152,17 @@
         push(m, i, mL, True)
     for i in range(CHUNKS):
         push(m, i, sib, True)
+
+    def product(src):
+        return dot(st[src], wb[pl.ds(pl.multiple_of(src * width, width), width), :])
+
+    for j in range(h2):
+        arrived(mL, j)
+        push(mL, j, mR)
+        push(mL, j, sib)
+        arrived(mR, j + h2)
+        push(mR, j + h2, mL)
+        push(mR, j + h2, sib)
 
     load_picks.wait()
     load_qe.wait()
@@ -166,22 +179,6 @@
     y_send(ym, ym_s, ym_r)
     z_send(qb.at[y], qz_s, qz_r)
 
-    load_st.wait()
-    load_w.wait()
-
-    def product(src):
-        return dot(st[src], wb[pl.ds(pl.multiple_of(src * width, width), width), :])
-
-    keys = product(m)
-
-    for j in range(h2):
-        arrived(mL, j)
-        push(mL, j, mR)
-        push(mL, j, sib)
-        arrived(mR, j + h2)
-        push(mR, j + h2, mL)
-        push(mR, j + h2, sib)
-
     pool_all = remote(pr.at[pl.ds(0, M8 - 1)], pr.at[pl.ds(0, M8 - 1)], pr_s, pr_r, (d, sib))
     pool_all.wait_recv()
     pooled = pp[c]
@@ -191,6 +188,11 @@
     pg[c, z] = jnp.concatenate([pooled, jnp.zeros((32 - half * p_dev, 128), F32)], axis=0).astype(BF16)
     z_send(pg.at[c], pg_s, pg_r)
 
+    load_st.wait()
+    load_w.wait()
+
+    keys = product(m)
+
     for j in range(h2):
         arrived(mL, j + h2)
         push(mL, j + h2, sib)
@@ -199,18 +201,6 @@
 
     z_all(gz, gz_s, gz_r).wait_recv()
     y_send(gb, gy_s, gy_r)
-
-    y_all(ym, ym_s, ym_r).wait_recv()
-    q8[...] = jnp.zeros_like(q8)
-    c4[...] = jnp.zeros_like(c4)
-    for i in range(Y):
-        c4[i:i + 1, :] = ym[i, pl.ds(8 + y, 1), :]
-        for j in range(nb):
-            q8[i:i + 1, j * 128:(j + 1) * 128] = ym[i, j:j + 1, :]
-    spread = jnp.concatenate(
-        [jnp.broadcast_to(c4[i:i + 1, :], (answers, 128)) for _ in range(128 // (Y * answers)) for i in range(Y)], axis=0
-    )
-    cm[...] = spread.T
 
     for j in range(CHUNKS):
         arrived(sib, j)
@@ -274,6 +264,18 @@
     ob[zlast] = lse[:, :128]
     lz_copy(zlast).start()
     lz[z] = lse[:, 128:]
+
+    y_all(ym, ym_s, ym_r).wait_recv()
+    q8[...] = jnp.zeros_like(q8)
+    c4[...] = jnp.zeros_like(c4)
+    for i in range(Y):
+        c4[i:i + 1, :] = ym[i, pl.ds(8 + y, 1), :]
+        for j in range(nb):
+            q8[i:i + 1, j * 128:(j + 1) * 128] = ym[i, j:j + 1, :]
+    spread = jnp.concatenate(
+        [jnp.broadcast_to(c4[i:i + 1, :], (answers, 128)) for _ in range(128 // (Y * answers)) for i in range(Y)], axis=0
+    )
+    cm[...] = spread.T
 
     z_all(qb.at[y], qz_s, qz_r).wait_recv()
     y_send(qb, qw_s, qw_r)
@@ -353,10 +355,11 @@
     lax.fori_loop(0, Z, spread_embed, 0)
     embed_all = qx[...].reshape(Z * 8, dr).astype(BF16)
     mine_only = jnp.where(lane == row + z * p_dev, 1.0, 0.0).astype(BF16)
+    dp_all[...] = jnp.zeros_like(dp_all)
     y_all(yb, yb_s, yb_r).wait_send()
     mb_all.wait_recv()
     delta = probs - jnp.sum(mb[...], axis=0)
-    dz[z] = delta
+    dz[z] = delta[:Y]
     z_send(dz, dz_s, dz_r)
     d1, d2 = split2(delta)
     grads = dot(d1, em[0]) + dot(d1, em[1]) + dot(d2, em[0])
@@ -374,7 +377,9 @@
     y_all(gyr, qy_s, qy_r).wait()
     gq_out[...] = gyr[0] + gyr[1] + gyr[2] + gyr[3]
     z_all(dz, dz_s, dz_r).wait()
-    b1, b2 = [dot_nt(mine_only, part).astype(BF16) for part in split2(dz[...].reshape(Z * 8, 128))]
+    for i in range(Z):
+        dp_all[i * 8:i * 8 + Y, :] = dz[i]
+    b1, b2 = [dot_nt(mine_only, part).astype(BF16) for part in split2(dp_all[...])]
     ge_out[...] = dot(b1, embed_all) + dot(b2, embed_all)
 
 
@@ -423,11 +428,12 @@
             pltpu.VMEM((Z, 8, 128), F32),
             pltpu.VMEM((Y, 8, 128), F32),
             pltpu.VMEM((mp, 8, 128), F32),
-            pltpu.VMEM((Z, 8, 128), F32),
+            pltpu.VMEM((Z, Y, 128), F32),
+            pltpu.VMEM((Z * 8, 128), F32),
             pltpu.VMEM((Y, 1, dr), F32),
             pltpu.VMEM((Y, 1, dr), F32),
             dma((7,)),
-            dma((28,)), dma((mp, CHUNKS)),
+            dma((7 * CHUNKS,)), dma((mp, CHUNKS)),
             *[dma] * 26,
         ],
         compiler_params=pltpu.CompilerParams(

time: 58.8 us -> 58.4 us (level)
  no operation moved by 1% of the time
where the time goes in v3:
time: 58.4 us; the launch traced here: 58.2 us
  Pallas kernels  54.9 us (94%)
  local copies, waits for them, and re-layouts  2.6 us (4%)
  between operations  0.64 us (1%)
    pallas_call x1, Pallas kernels, body(): pl.pallas_call(functools.partial(kernel, Z, length, all_cols // HD), out_...  54.9 us
    unnamed x2, local copies, waits for them, and re-layouts  2.6 us

profile of v3, /device:TPU:1, one launch (start us, length us, event | category | flops | bytes accessed | tf_op | source)
XLA Modules:
  0.0 58.2 jit_solution(8811852752602478490)
XLA Ops:
  0.6 54.9 %shard_map.86 = (f32[8,768]{1,0:T(8,128)}, f32[1,768]{1,0:T(1,128)}) custom-call(s32[1,16]{1,0:T(1,128)} %picks_hbm.1, bf16[1,768]{1,0:T(2,128)(2,1)} %qe_hbm.1, bf16[8,2048]{1,0:T(8,128)(2,1)} %bitcast.3, bf16[256,512]{1,0:T(8,128)(2,1)} %bitcast.2, bf16[8,4,768]{2,1,0:T(4,128)(2,1)} %retr_hbm.1, bf16[4096,256]{1,0:T(8,128)(2,1)} %kw.1, bf16[768,768]{1,0:T(8,128)(2,1)} %rw.1), custom_call_target="tpu_custom_call" | custom-call | tf_op jit(solution)/shard_map/pallas_call | solution.py:400
  55.6 1.3 %copy.11 = f32[8,768]{1,0:T(8,128)} copy(f32[8,768]{1,0:T(8,128)} %get-tuple-element.4) | data formatting | bytes 49152
  56.9 1.3 %copy.12 = f32[1,768]{1,0:T(1,128)} copy(f32[1,768]{1,0:T(1,128)} %get-tuple-element.5) | data formatting | bytes 6144

commit v4 on v3

--- a/solution.py
+++ b/solution.py
@@ -13,7 +13,7 @@
 F32 = jnp.float32
 BF16 = jnp.bfloat16
 NT = (((1,), (1,)), ((), ()))
-CHUNKS = 4
+CHUNKS = 2
 Y = 4
 X = 4
 

time: 58.4 us -> 58.2 us (level)
  no operation moved by 1% of the time
where the time goes in v4:
time: 58.2 us; the launch traced here: 58 us
  Pallas kernels  54.7 us (94%)
  local copies, waits for them, and re-layouts  2.6 us (4%)
  between operations  0.64 us (1%)
    pallas_call x1, Pallas kernels, body(): pl.pallas_call(functools.partial(kernel, Z, length, all_cols // HD), out_...  54.7 us
    unnamed x2, local copies, waits for them, and re-layouts  2.6 us

profile of v4, /device:TPU:1, one launch (start us, length us, event | category | flops | bytes accessed | tf_op | source)
XLA Modules:
  0.0 58.0 jit_solution(16034622359361139293)
XLA Ops:
  0.6 54.7 %shard_map.86 = (f32[8,768]{1,0:T(8,128)}, f32[1,768]{1,0:T(1,128)}) custom-call(s32[1,16]{1,0:T(1,128)} %picks_hbm.1, bf16[1,768]{1,0:T(2,128)(2,1)} %qe_hbm.1, bf16[8,2048]{1,0:T(8,128)(2,1)} %bitcast.3, bf16[256,512]{1,0:T(8,128)(2,1)} %bitcast.2, bf16[8,4,768]{2,1,0:T(4,128)(2,1)} %retr_hbm.1, bf16[4096,256]{1,0:T(8,128)(2,1)} %kw.1, bf16[768,768]{1,0:T(8,128)(2,1)} %rw.1), custom_call_target="tpu_custom_call" | custom-call | tf_op jit(solution)/shard_map/pallas_call | solution.py:400
  55.4 1.3 %copy.11 = f32[8,768]{1,0:T(8,128)} copy(f32[8,768]{1,0:T(8,128)} %get-tuple-element.4) | data formatting | bytes 49152
  56.7 1.3 %copy.12 = f32[1,768]{1,0:T(1,128)} copy(f32[1,768]{1,0:T(1,128)} %get-tuple-element.5) | data formatting | bytes 6144
